TPU v7x, 256 devices: a whole 4x4x8 slice. The times are simulated.
256 devices in a mesh: section: 8 (over y_lo, x), seq: 32 (over y_hi, z, core).
Axes of the slice: x: 4, y: 4 (y_hi: 2, y_lo: 2; y = y_hi * 2 + y_lo), z: 8, core: 2. Of those that a mesh axis runs over, the one named last changes fastest.
Arguments:
- stream: bfloat16 [8, 4096, 3584], P('section', 'seq'), may hold values from -6 to 6
- keys: bfloat16 [8, 4096, 3584], P('section', 'seq'), may hold values from -400 to 400
- values: bfloat16 [8, 4096, 3584], P('section', 'seq'), may hold values from -6 to 6
- bc: bfloat16 [8, 4096, 128], P('section', 'seq'), may hold values from -3 to 3
- rates: float32 [8, 4096, 56], P('section', 'seq'), may hold values from 0 to 1, as said below
- dskip: float32 [8, 56], P('section'), may hold values from 1 to 8
- norm_gain: float32 [8, 3584], P('section'), may hold values from 0.25 to 1.75
- seg_ids: int32 [8, 4096], P('section', 'seq'), may hold values from 0 to 31, never falling along the last dimension, each value on 1 to 512 neighbouring positions
Outputs:
- next_stream: bfloat16 [8, 4096, 3584], P('section', 'seq')
Inputs may be any that keep to these rules, and one draw needn't show every extreme that they name: `seg_ids`: each document covers at most 512 consecutive positions, and in every row some document covers exactly that many. `rates`: Positive.
All inputs are finite; a program needn't handle non-finite values.
Results may differ from a plain program's by a relative error of at most 0.0085.
Values may be sent and summed in bfloat16 or wider, within the bound.
A program may use at most 128 MiB of HBM per device.

v0:
```python
import jax
import jax.numpy as jnp
from jax import lax
from jax.sharding import PartitionSpec as P

SSD_ATTN_GROUPS = 56
HEAD_P = 64
NSTATE = 64
ATT_HEADS = 16
ATT_DIM = 224
BACK = 4


def prefix(part, axis, combine, identity):
    place = lax.axis_index(axis)
    gathered = jax.tree.map(lambda a: lax.all_gather(a, axis), part)
    state = jax.tree.map(lambda a, e: jnp.zeros_like(a) + jnp.asarray(e, a.dtype), part, identity)

    def one(hop, state):
        return combine(
            state, jax.tree.map(lambda a: lax.dynamic_index_in_dim(a, hop, 0, False), gathered)
        )

    return lax.fori_loop(0, place, one, state)


def from_behind(array, axis, by):
    peers = lax.axis_size(axis)
    pairs = [(i, i + by) for i in range(peers) if 0 <= i + by < peers]
    return lax.ppermute(array, axis, pairs)


def shifted(array, axis, by):
    peers = lax.axis_size(axis)
    return lax.ppermute(array, axis, [(i, (i + by) % peers) for i in range(peers)])


def local_state(x_rows, bmat, cum):
    rows = x_rows.shape[0]
    xh = x_rows.reshape(rows, SSD_ATTN_GROUPS, HEAD_P)
    total = cum[-1]
    weight = jnp.exp(-(total[None, :] - cum))
    weighted = (xh.astype(jnp.float32) * weight[:, :, None]).reshape(rows, HIDDEN_W_LOCAL(x_rows))
    local = jnp.dot(weighted.T, bmat.astype(jnp.float32), precision=lax.Precision.HIGHEST)
    return (jnp.exp(-total), local.reshape(SSD_ATTN_GROUPS, HEAD_P * NSTATE))


def HIDDEN_W_LOCAL(x_rows):
    return x_rows.shape[1]


def combine_state(earlier, later):
    return (earlier[0] * later[0], later[1] + later[0][:, None] * earlier[1])


def body(stream, keys, values, bc, rates, dskip, norm_gain, seg_ids):
    x_rows = stream[0]
    rows, width = x_rows.shape
    xh = x_rows.reshape(rows, SSD_ATTN_GROUPS, HEAD_P)
    bmat = bc[0][:, :NSTATE]
    cmat = bc[0][:, NSTATE:]
    cum = jnp.cumsum(rates[0], axis=0)
    dtot, local = local_state(x_rows, bmat, cum)
    identity = (
        jnp.ones((SSD_ATTN_GROUPS,), jnp.float32),
        jnp.zeros((SSD_ATTN_GROUPS, HEAD_P * NSTATE), jnp.float32),
    )
    carried_in = prefix((dtot, local), "seq", combine_state, identity)
    state_in = carried_in[1]
    inner_dot = jnp.dot(cmat, bmat.T, preferred_element_type=jnp.float32)
    cum_t = cum.T
    gap = cum_t[:, :, None] - cum_t[:, None, :]
    lower = jnp.arange(rows)[:, None] >= jnp.arange(rows)[None, :]
    decay = jnp.where(lower[None], jnp.exp(-jnp.where(lower[None], gap, 0.0)), 0.0)
    mixing = (inner_dot[None] * decay).astype(jnp.bfloat16)
    inner = jnp.einsum("hts,shp->thp", mixing, xh, preferred_element_type=jnp.float32)
    flat_state = state_in.reshape(width, NSTATE)
    carried = jnp.dot(cmat.astype(jnp.float32), flat_state.T, precision=lax.Precision.HIGHEST)
    carried = carried.reshape(rows, SSD_ATTN_GROUPS, HEAD_P) * jnp.exp(-cum)[:, :, None]
    y_full = inner + carried + dskip[0][None, :, None] * xh.astype(jnp.float32)
    meansq = jnp.mean(y_full * y_full, axis=-1, keepdims=True)
    u_rows = (
        (y_full * lax.rsqrt(meansq + 1e-05)).reshape(rows, width) * norm_gain[0][None, :]
    ).astype(jnp.bfloat16)
    own_keys = keys[0]
    own_values = values[0]
    own_seg = seg_ids[0]
    remote = []
    for distance in range(1, BACK + 1):
        remote.append(from_behind((own_keys, own_values, own_seg), "seq", distance))
    index = lax.axis_index("seq")
    offsets = jnp.arange(rows, dtype=jnp.int32)
    key_parts = []
    value_parts = []
    seg_parts = []
    pos_parts = []
    for distance in range(BACK, 0, -1):
        piece = remote[distance - 1]
        key_parts.append(piece[0])
        value_parts.append(piece[1])
        seg_parts.append(piece[2])
        pos_parts.append((index - distance) * rows + offsets)
    key_parts.append(own_keys)
    value_parts.append(own_values)
    seg_parts.append(own_seg)
    pos_parts.append(index * rows + offsets)
    keys_win = jnp.concatenate(key_parts, axis=0)
    values_win = jnp.concatenate(value_parts, axis=0)
    seg_k = jnp.concatenate(seg_parts, axis=0)
    kpos = jnp.concatenate(pos_parts, axis=0)
    qpos = index * rows + offsets
    query = u_rows.reshape(rows, ATT_HEADS, ATT_DIM)
    key_h = keys_win.reshape(-1, ATT_HEADS, ATT_DIM)
    val_h = values_win.reshape(-1, ATT_HEADS, ATT_DIM)
    scores = jnp.einsum(
        "thd,khd->htk", query, key_h, preferred_element_type=jnp.float32
    ) * ATT_DIM ** (-0.5)
    allowed = (
        (kpos[None, :] >= 0)
        & (kpos[None, :] <= qpos[:, None])
        & (seg_k[None, :] == own_seg[:, None])
    )
    scores = jnp.where(allowed[None], scores, -1e30)
    top = jnp.max(scores, axis=-1, keepdims=True)
    expo = jnp.where(allowed[None], jnp.exp(scores - top), 0.0)
    totals = jnp.sum(expo, axis=-1)
    probs = expo.astype(jnp.bfloat16)
    attended = (
        jnp.einsum("htk,khd->thd", probs, val_h, preferred_element_type=jnp.float32)
        / totals.T[:, :, None]
    )
    attended = attended.reshape(rows, width)
    summed = x_rows.astype(jnp.float32) + u_rows.astype(jnp.float32) + attended
    out_rows = summed.astype(jnp.bfloat16)
    return shifted(out_rows[None], "section", 1)


def solution(mesh):
    in_specs = (
        P("section", "seq", None),
        P("section", "seq", None),
        P("section", "seq", None),
        P("section", "seq", None),
        P("section", "seq", None),
        P("section", None),
        P("section", None),
        P("section", "seq"),
    )
    out_specs = P("section", "seq", None)
    return jax.shard_map(body, mesh=mesh, in_specs=in_specs, out_specs=out_specs, check_vma=False)
```

profile of v0, /device:TPU:249, one launch (start us, length us, event | category | flops | bytes accessed | tf_op | source)
XLA Modules:
  0.0 465.2 jit_solution(16328989460574676309)
XLA Ops:
  7.7 1.6 copy.45
  10.5 1.5 all_gather_reshape.3
  18.8 121.3 %collective-permute-done.4 = s32[128]{0:T(128)S(1)} collective-permute-done((s32[128]{0:T(128)S(1)}, s32[128]{0:T(128)S(1)}, u32[]{:S(2)}, u32[]{:S(2)}) %collective-permute-start.4) | collective-permute-done | bytes 544 | tf_op jit(solution)/shard_map/ppermute | solution.py:30
  142.8 2.1 collective-permute-done.6
  151.4 1.6 copy.62
  153.0 1.6 copy.57
  154.8 184.5 %all-gather = f32[32,1,56]{2,1,0:T(1,128)S(1)} all-gather(f32[1,1,56]{2,1,0:T(1,128)S(1)} %get-tuple-element.62), channel_id=1, replica_groups=mesh['section'=8,'seq'=32] {'seq'}, dimensions={0}, use_global_device_ids=true | all-gather | bytes 7392 | tf_op jit(solution)/shard_map/all_gather | solution.py:16
  339.6 2.2 copy.58
  341.8 2.2 copy.59
  344.0 2.2 copy.60
  346.2 2.2 copy.61
  348.5 2.2 copy.53
  350.7 2.2 copy.54
  352.9 2.2 copy.55
  355.1 2.2 copy.56
  357.4 2.4 constant_dynamic-update-slice_fusion.11
  359.7 2.2 constant_dynamic-update-slice_fusion.4
  370.5 46.0 %while.12 = (s32[]{:T(128)}, f32[56,4096]{1,0:T(8,128)S(1)}, s32[]{:T(128)}, f32[32,56,4096]{2,1,0:T(8,128)}, f32[32,56]{1,0:T(8,128)S(1)}, /*index=5*/s32[]{:T(128)}, s32[]{:T(128)}, s32[]{:T(128)}) while((s32[]{:T(128)}, f32[56,4096]{1,0:T(8,128)S(1)}, s32[]{:T(128)}, f32[32,56,4096]{2,1,0:T(8,128)}, f32[32,56]{1,0:T(8,128)S(1)}, ...), condition=%wide.region_2.3_spmd, body=%wide.region_1.2_spmd.sunk | while | flops 458757 | bytes 2753311 | solution.py:24
  370.5 1.4 bitcast_add_fusion.3
  372.0 1.4 bitcast_add_fusion.3
  373.5 1.4 bitcast_add_fusion.3
  375.0 1.4 bitcast_add_fusion.3
  376.4 1.4 bitcast_add_fusion.3
  377.9 1.4 bitcast_add_fusion.3
  379.4 1.4 bitcast_add_fusion.3
  380.9 1.4 bitcast_add_fusion.3
  382.4 1.4 bitcast_add_fusion.3
  383.8 1.4 bitcast_add_fusion.3
  385.3 1.4 bitcast_add_fusion.3
  386.8 1.4 bitcast_add_fusion.3
  388.3 1.4 bitcast_add_fusion.3
  389.8 1.4 bitcast_add_fusion.3
  391.2 1.4 bitcast_add_fusion.3
  392.7 1.4 bitcast_add_fusion.3
  394.2 1.4 bitcast_add_fusion.3
  395.7 1.4 bitcast_add_fusion.3
  397.1 1.4 bitcast_add_fusion.3
  398.6 1.4 bitcast_add_fusion.3
  400.1 1.4 bitcast_add_fusion.3
  401.6 1.4 bitcast_add_fusion.3
  403.1 1.4 bitcast_add_fusion.3
  416.5 2.0 reshape.240
  418.5 2.5 fusion.27
  421.1 1.7 multiply_reduce_fusion
  423.0 3.5 fusion.22
  426.6 2.7 fusion.33
  429.3 3.7 bitcast_divide_fusion
  435.0 22.1 %collective-permute-done.12 = bf16[1,128,3584]{1,2,0:T(8,128)(2,1)S(1)} collective-permute-done((bf16[1,128,3584]{1,2,0:T(8,128)(2,1)S(1)}, bf16[1,128,3584]{1,2,0:T(8,128)(2,1)S(1)}, u32[]{:S(2)}, u32[]{:S(2)}) %collective-permute-start.12) | collective-permute-done | bytes 917536 | tf_op jit(solution)/shard_map/ppermute | solution.py:35
  (130 shorter events, 42.3 us)
Async XLA Ops:
  6.5 2.8 copy-start.8
  6.5 363.9 %all-gather.3.cloned.1.call-start = ((), (), s32[]{:S(2)}) async-start(), calls=%async_computation | async-start | bytes 30277632 | tf_op jit(solution)/shard_map/all_gather | solution.py:16
  9.4 6.5 %copy-start.10 = (s32[1,128]{1,0:T(1,128)S(1)}, s32[1,128]{1,0:T(1,128)}, u32[]{:S(2)}) copy-start(s32[1,128]{1,0:T(1,128)} %param.17) | copy-start | bytes 1540
  10.4 144.2 %copy-start.9 = (f32[1,3584]{1,0:T(1,128)S(1)}, f32[1,3584]{1,0:T(1,128)}, u32[]{:S(2)}) copy-start(f32[1,3584]{1,0:T(1,128)} %param.16) | copy-start | bytes 43012
  12.0 135.4 %collective-permute-start.8 = (bf16[128,3584]{1,0:T(8,128)(2,1)}, bf16[128,3584]{1,0:T(8,128)(2,1)S(1)}, u32[]{:S(2)}, u32[]{:S(2)}) collective-permute-start(bf16[128,3584]{1,0:T(8,128)(2,1)} %bitcast.76), channel_id=1, source_target_pairs={{0,4},{1,5},{2,6},{3,7},{4,8},{5,9},{6,10},{7,11},{8,12},{9,13},{1... | collective-permute-start | bytes 2752520 | tf_op jit(solution)/shard_map/ppermute | solution.py:30
  13.3 135.4 %collective-permute-start.9 = (bf16[128,3584]{1,0:T(8,128)(2,1)}, bf16[128,3584]{1,0:T(8,128)(2,1)S(1)}, u32[]{:S(2)}, u32[]{:S(2)}) collective-permute-start(bf16[128,3584]{1,0:T(8,128)(2,1)} %bitcast.77), channel_id=1, source_target_pairs={{0,3},{1,4},{2,5},{3,6},{4,7},{5,8},{6,9},{7,10},{8,11},{9,12},{10... | collective-permute-start | bytes 2752520 | tf_op jit(solution)/shard_map/ppermute | solution.py:30
  14.6 135.5 %collective-permute-start.10 = (bf16[128,3584]{1,0:T(8,128)(2,1)}, bf16[128,3584]{1,0:T(8,128)(2,1)}, u32[]{:S(2)}, u32[]{:S(2)}) collective-permute-start(bf16[128,3584]{1,0:T(8,128)(2,1)} %bitcast.78), channel_id=1, source_target_pairs={{0,2},{1,3},{2,4},{3,5},{4,6},{5,7},{6,8},{7,9},{8,10},{9,11},{10,... | collective-permute-start | bytes 2752520 | tf_op jit(solution)/shard_map/ppermute | solution.py:30
  15.9 124.2 %collective-permute-start.4 = (s32[128]{0:T(128)S(1)}, s32[128]{0:T(128)S(1)}, u32[]{:S(2)}, u32[]{:S(2)}) collective-permute-start(s32[128]{0:T(128)S(1)} %bitcast.90), channel_id=1, source_target_pairs={{0,4},{1,5},{2,6},{3,7},{4,8},{5,9},{6,10},{7,11},{8,12},{9,13},{1... | collective-permute-start | bytes 1544 | tf_op jit(solution)/shard_map/ppermute | solution.py:30
  17.2 124.2 %collective-permute-start.5 = (s32[128]{0:T(128)S(1)}, s32[128]{0:T(128)S(1)}, u32[]{:S(2)}, u32[]{:S(2)}) collective-permute-start(s32[128]{0:T(128)S(1)} %bitcast.91), channel_id=1, source_target_pairs={{0,3},{1,4},{2,5},{3,6},{4,7},{5,8},{6,9},{7,10},{8,11},{9,12},{10... | collective-permute-start | bytes 1544 | tf_op jit(solution)/shard_map/ppermute | solution.py:30
  140.1 4.7 %collective-permute-start.6 = (s32[128]{0:T(128)S(1)}, s32[128]{0:T(128)S(1)}, u32[]{:S(2)}, u32[]{:S(2)}) collective-permute-start(s32[128]{0:T(128)S(1)} %bitcast.92), channel_id=1, source_target_pairs={{0,2},{1,3},{2,4},{3,5},{4,6},{5,7},{6,8},{7,9},{8,10},{9,11},{10,... | collective-permute-start | bytes 1544 | tf_op jit(solution)/shard_map/ppermute | solution.py:30
  141.4 4.7 %collective-permute-start.7 = (s32[128]{0:T(128)S(1)}, s32[128]{0:T(128)S(1)}, u32[]{:S(2)}, u32[]{:S(2)}) collective-permute-start(s32[128]{0:T(128)S(1)} %bitcast.93), channel_id=1, source_target_pairs={{0,1},{1,2},{2,3},{3,4},{4,5},{5,6},{6,7},{7,8},{8,9},{9,10},{10,1... | collective-permute-start | bytes 1544 | tf_op jit(solution)/shard_map/ppermute | solution.py:30
  144.8 201.4 %collective-permute-start.11 = (bf16[128,3584]{1,0:T(8,128)(2,1)}, bf16[128,3584]{1,0:T(8,128)(2,1)}, u32[]{:S(2)}, u32[]{:S(2)}) collective-permute-start(bf16[128,3584]{1,0:T(8,128)(2,1)} %bitcast.79), channel_id=1, source_target_pairs={{0,1},{1,2},{2,3},{3,4},{4,5},{5,6},{6,7},{7,8},{8,9},{9,10},{10,1... | collective-permute-start | bytes 2752520 | tf_op jit(solution)/shard_map/ppermute | solution.py:30
  146.1 202.3 %collective-permute-start = (bf16[128,3584]{1,0:T(8,128)(2,1)}, bf16[128,3584]{1,0:T(8,128)(2,1)}, u32[]{:S(2)}, u32[]{:S(2)}) collective-permute-start(bf16[128,3584]{1,0:T(8,128)(2,1)} %bitcast.80), channel_id=1, source_target_pairs={{0,4},{1,5},{2,6},{3,7},{4,8},{5,9},{6,10},{7,11},{8,12},{9,13},{1... | collective-permute-start | bytes 2752520 | tf_op jit(solution)/shard_map/ppermute | solution.py:30
  147.4 5.5 %copy-start.6 = (bf16[128,3584]{1,0:T(8,128)(2,1)}, bf16[128,3584]{1,0:T(8,128)(2,1)S(1)}, u32[]{:S(2)}) copy-start(bf16[128,3584]{1,0:T(8,128)(2,1)S(1)} %collective-permute-done.8) | copy-start | bytes 2752516
  147.4 203.2 %collective-permute-start.1 = (bf16[128,3584]{1,0:T(8,128)(2,1)}, bf16[128,3584]{1,0:T(8,128)(2,1)}, u32[]{:S(2)}, u32[]{:S(2)}) collective-permute-start(bf16[128,3584]{1,0:T(8,128)(2,1)} %bitcast.81), channel_id=1, source_target_pairs={{0,3},{1,4},{2,5},{3,6},{4,7},{5,8},{6,9},{7,10},{8,11},{9,12},{10... | collective-permute-start | bytes 2752520 | tf_op jit(solution)/shard_map/ppermute | solution.py:30
  148.7 2.6 copy-start.7
  148.7 204.2 %collective-permute-start.2 = (bf16[128,3584]{1,0:T(8,128)(2,1)}, bf16[128,3584]{1,0:T(8,128)(2,1)}, u32[]{:S(2)}, u32[]{:S(2)}) collective-permute-start(bf16[128,3584]{1,0:T(8,128)(2,1)} %bitcast.82), channel_id=1, source_target_pairs={{0,2},{1,3},{2,4},{3,5},{4,6},{5,7},{6,8},{7,9},{8,10},{9,11},{10,... | collective-permute-start | bytes 2752520 | tf_op jit(solution)/shard_map/ppermute | solution.py:30
  150.1 205.1 %collective-permute-start.3 = (bf16[128,3584]{1,0:T(8,128)(2,1)}, bf16[128,3584]{1,0:T(8,128)(2,1)}, u32[]{:S(2)}, u32[]{:S(2)}) collective-permute-start(bf16[128,3584]{1,0:T(8,128)(2,1)} %bitcast.83), channel_id=1, source_target_pairs={{0,1},{1,2},{2,3},{3,4},{4,5},{5,6},{6,7},{7,8},{8,9},{9,10},{10,1... | collective-permute-start | bytes 2752520 | tf_op jit(solution)/shard_map/ppermute | solution.py:30
  357.3 4.6 copy-start.1
  357.4 5.7 %copy-start = (bf16[128,3584]{0,1:T(8,128)(2,1)S(1)}, bf16[128,3584]{0,1:T(8,128)(2,1)}, u32[]{:S(2)}) copy-start(bf16[128,3584]{0,1:T(8,128)(2,1)} %copy.60) | copy-start | bytes 2752516
  357.4 6.7 %copy-start.2 = (bf16[128,3584]{0,1:T(8,128)(2,1)S(1)}, bf16[128,3584]{0,1:T(8,128)(2,1)}, u32[]{:S(2)}) copy-start(bf16[128,3584]{0,1:T(8,128)(2,1)} %copy.61) | copy-start | bytes 2752516
  362.0 4.2 copy-start.3
  363.0 4.3 copy-start.4
  364.1 4.2 copy-start.5
  416.5 4.6 copy-start.11
  433.6 23.4 %collective-permute-start.12 = (bf16[1,128,3584]{1,2,0:T(8,128)(2,1)S(1)}, bf16[1,128,3584]{1,2,0:T(8,128)(2,1)S(1)}, u32[]{:S(2)}, u32[]{:S(2)}) collective-permute-start(bf16[1,128,3584]{1,2,0:T(8,128)(2,1)S(1)} %fusion.9), channel_id=1, source_target_pairs={{0,32},{32,64},{64,96},{96,128},{128,160},{160,192},{192,224},{224... | collective-permute-start | bytes 2752520 | tf_op jit(solution)/shard_map/ppermute | solution.py:35
Sparse Core Ops, SparseCore 0:
  12.1 320.2 all-gather.2
where the time goes:
time: 467 us; the launch traced here: 465 us
  blocking collectives  185 us (40%)
  waiting for transfers between devices  146 us (31%)
  other arithmetic  48.5 us (10%)
  local copies, waits for them, and re-layouts  42 us (9%)
  starting transfers between devices  16.8 us (4%)
  between operations  13.9 us (3%)
  matrix products  12.7 us (3%)
    all_gather x1, blocking collectives, prefix(): gathered = jax.tree.map(lambda a: lax.all_gather(a, axis), part)  185 us
    ppermute x12, waiting for transfers between devices, from_behind(): return lax.ppermute(array, axis, pairs)  123 us
    add x31, other arithmetic, combine_state(): return (earlier[0] * later[0], later[1] + later[0][:, None] * earlier[1])  44.4 us
    ppermute x1, waiting for transfers between devices, shifted(): lax.ppermute(array, axis, [(i, (i + by) % peers) for i in range(peers)])  22.1 us
    ppermute x8, local copies, waits for them, and re-layouts, from_behind(): return lax.ppermute(array, axis, pairs)  17.8 us
    unnamed x39, local copies, waits for them, and re-layouts  15.7 us
    ppermute x12, starting transfers between devices, from_behind(): return lax.ppermute(array, axis, pairs)  15.5 us
  transfers between devices with their start and end apart: 14, of which 3 were waited for; matrix products, arithmetic and copies ran while one was open for 7% of the time, Pallas kernels for 0%

commit v1 on v0

v1 whole, which is shorter than its diff:
```python
import functools

import jax
import jax.numpy as jnp
from jax import lax
from jax.experimental import pallas as pl
from jax.experimental.pallas import tpu as pltpu
from jax.sharding import PartitionSpec as P

ROWS = 128
HEAD_P = 64
NSTATE = 64
ATT_DIM = 224
BACK = 4
LANES = 128
QUAD = 4 * ATT_DIM
TILES = QUAD // LANES
SPAN = (BACK + 1) * ROWS
LOWEST = -1e20
MASKED = -1e30
WINDOWS = ((0, 256), (128, 384), (384, 384), (640, 256))
MODES = ("q", "q", "q", "k")
MESH = pl.DeviceIdType.MESH
F32 = jnp.float32
BF16 = jnp.bfloat16


def iota(shape, dim):
    return lax.broadcasted_iota(jnp.int32, shape, dim)


def halves(a):
    hi = a.astype(BF16)
    return hi, (a - hi.astype(F32)).astype(BF16)


def dot(a, b, dims=((1,), (0,)), precision=None):
    return lax.dot_general(a, b, (dims, ((), ())), precision=precision, preferred_element_type=F32)


def kernel(
    modes, sections, peers,
    x_ref, k_ref, v_ref, bc_ref, rate_ref, dskip_ref, gain_ref, seg_ref,
    out_ref,
    cumx, y0, dsx, gmat, s_own, s_sib, t_out, t_in, p_out, p_in, u_all, seg_out, seg_k, seg_q, bias_k, bias_q,
    kv_buf, q_buf, part_o, part_s, sib_o, sib_s, f_out, f_outs, f_in, f_ins, n_out, n_outs, n_in, n_ins, res,
    seg_sem, s_sem, t_ssem, t_rsem, p_ssem, p_rsem, h_sem, kv_sem, q_sem, sib_sem, chain_sem, out_sem,
):
    quads = len(modes)
    qs = [q for q in range(quads) if modes[q] == "q"]
    ks = [q for q in range(quads) if modes[q] == "k"]
    slices = quads * TILES
    chips = peers // 2
    owned = (slices + 1) // 2
    sec = lax.axis_index("section")
    me = lax.axis_index("seq")
    core = me % 2
    chip = me // 2
    sibling = me + 1 - 2 * core
    first = core == 0
    second = core == 1
    up2, up4 = me + 2 < peers, me + 4 < peers
    dn2, dn4 = me >= 2, me >= 4
    after_first = chip > 0
    before_last = chip < chips - 1

    def seq_dev(index):
        return (sec, index)

    def remote(src, dst, send, recv, device):
        return pltpu.make_async_remote_copy(
            src_ref=src, dst_ref=dst, send_sem=send, recv_sem=recv, device_id=device, device_id_type=MESH
        )

    def at(cond, fn):
        if cond is True:
            fn()
        else:
            pl.when(cond)(fn)

    pending = []

    def send(cond, copy):
        at(cond, copy.start)
        pending.append((cond, copy))

    def lane(j):
        return pl.ds(pl.multiple_of(j * LANES, LANES), LANES)

    def quad_lanes(q):
        return pl.ds(q * QUAD, QUAD)

    barrier = pltpu.get_barrier_semaphore()
    greeted = 0
    for hop in (1, sections - 1):
        pl.semaphore_signal(barrier, inc=1, device_id=((sec + hop) % sections, me), device_id_type=MESH)
        greeted += 1
    hops = sorted({2 * m for m in range(1, chips)} | {1, 3, peers - 3, peers - 1})
    for hop in hops:
        pl.semaphore_signal(barrier, inc=1, device_id=seq_dev((me + hop) % peers), device_id_type=MESH)
        greeted += 1
    pl.semaphore_wait(barrier, greeted)

    seg_out[...] = jnp.broadcast_to(seg_ref[...].astype(F32), (8, LANES))
    seg_copies = []
    for d in range(1, BACK + 1):
        fwd = remote(seg_out, seg_k.at[d - 1], seg_sem.at[0, d - 1], seg_sem.at[1, d - 1], seq_dev((me + d) % peers))
        bwd = remote(
            seg_out, seg_q.at[d - 1], seg_sem.at[2, d - 1], seg_sem.at[3, d - 1], seq_dev((me + peers - d) % peers)
        )
        send(True, fwd)
        send(True, bwd)
        seg_copies += [fwd, bwd]

    def kv_parts(q):
        n = ks.index(q)
        return [(n, w, (k_ref, v_ref)[w]) for w in range(2)]

    def kv_slot(n, w, d):
        return kv_buf.at[n, w, pl.ds(d * ROWS, ROWS)]

    def kv_copy(n, w, src, d, kind, device):
        return remote(src, kv_slot(n, w, d), kv_sem.at[0, n, w, kind], kv_sem.at[1, n, w, kind], seq_dev(device))

    right = (me + 2) % peers
    left = (me + peers - 2) % peers

    def kv_start(q):
        for n, w, src in kv_parts(q):
            own = src.at[:, quad_lanes(q)]
            send(up2, kv_copy(n, w, own, 2, 0, right))
            send(first, kv_copy(n, w, own, 1, 2, sibling))

    def kv_near(q):
        for n, w, _ in kv_parts(q):
            near = kv_slot(n, w, 2)
            at(dn2, kv_copy(n, w, near, 2, 0, right).wait_recv)
            send(dn2 & up2, kv_copy(n, w, near, 4, 1, right))
            send(dn2 & first, kv_copy(n, w, near, 3, 3, sibling))
            send(dn2 & second, kv_copy(n, w, near, 1, 2, sibling))

    def kv_far(q):
        for n, w, _ in kv_parts(q):
            far = kv_slot(n, w, 4)
            at(dn4, kv_copy(n, w, far, 4, 1, right).wait_recv)
            send(dn4 & second, kv_copy(n, w, far, 3, 3, sibling))

    def kv_last(q):
        for n, w, _ in kv_parts(q):
            at(second | dn2, kv_copy(n, w, kv_slot(n, w, 1), 1, 2, sibling).wait_recv)
            at((second & dn2) | (first & dn4), kv_copy(n, w, kv_slot(n, w, 3), 3, 3, sibling).wait_recv)

    for q in ks:
        kv_start(q)
    for n in range(len(ks)):
        for w in range(2):
            for d in range(1, BACK + 1):

                def blank(n=n, w=w, d=d):
                    kv_buf[n, w, pl.ds(d * ROWS, ROWS)] = jnp.zeros((ROWS, QUAD), BF16)

                at(me < d, blank)

    row_i, col_i = iota((ROWS, LANES), 0), iota((ROWS, LANES), 1)
    heads = rate_ref.shape[1]
    cum = dot((row_i >= col_i).astype(F32), rate_ref[...], precision=lax.Precision.HIGHEST)
    skip8 = jnp.broadcast_to(dskip_ref[...], (8, heads))
    bc = bc_ref[...]
    bc_t = bc.astype(F32).T
    b_t = bc_t[:NSTATE].astype(BF16)
    b_t2 = jnp.concatenate([b_t, b_t], axis=1)
    for q in range(quads):
        spread = (iota((heads, QUAD), 1) // HEAD_P + q * (QUAD // HEAD_P) == iota((heads, QUAD), 0)).astype(F32)
        cumx[:, quad_lanes(q)] = dot(cum, spread, precision=lax.Precision.HIGHEST)
        dsx[:, quad_lanes(q)] = dot(skip8, spread, precision=lax.Precision.HIGHEST)

        @pl.loop(q * TILES, (q + 1) * TILES)
        def _(j):
            sl = lane(j)
            cx = cumx[:, sl]
            total = cx[ROWS - 1 :]
            hi, lo = halves(x_ref[:, sl].astype(F32) * jnp.exp(cx - total))
            s_own[0:NSTATE, sl] = dot(b_t2, jnp.concatenate([hi, lo], axis=0))
            s_own[NSTATE : NSTATE + 8, sl] = jnp.broadcast_to(total, (8, LANES))

        send(
            True,
            remote(
                s_own.at[:, quad_lanes(q)], s_sib.at[:, quad_lanes(q)], s_sem.at[0, q], s_sem.at[1, q],
                seq_dev(sibling),
            ),
        )

    def t_copy(j):
        return remote(t_out.at[j // 2], t_in.at[chip], t_ssem.at[j // 2], t_rsem.at[chip], seq_dev(j))

    def states_out(q):
        quad = quad_lanes(q)
        remote(s_own.at[:, quad], s_sib.at[:, quad], s_sem.at[0, q], s_sem.at[1, q], seq_dev(sibling)).wait_recv()

        @pl.loop(q * TILES, (q + 1) * TILES)
        def _(j):
            @pl.when((j % 2 == core) & before_last)
            def _():
                sl = lane(j)
                own, sib = s_own[0:NSTATE, sl], s_sib[0:NSTATE, sl]
                own_tot, sib_tot = s_own[NSTATE : NSTATE + 1, sl], s_sib[NSTATE : NSTATE + 1, sl]
                early = jnp.where(first, own, sib)
                late = jnp.where(first, sib, own)
                late_tot = jnp.where(first, sib_tot, own_tot)
                both = jnp.exp(-late_tot) * early + late
                total = own_tot + sib_tot
                hi = total.astype(BF16).astype(F32)
                mid = (total - hi).astype(BF16).astype(F32)
                low = total - hi - mid
                place = iota((16, LANES), 0)
                tail = jnp.where(place == 0, hi, jnp.where(place == 1, mid, jnp.where(place == 2, low, 0.0)))
                block = jnp.concatenate([both, tail], axis=0).astype(BF16)

                @pl.when(j != me)
                def _():
                    t_out[j // 2] = block
                    t_copy(j).start()

                @pl.when(j == me)
                def _():
                    t_in[chip] = block

    def p_copy(owner, target):
        sl = lane(owner)
        return remote(
            p_out.at[target // 2], p_in.at[:, sl], p_ssem.at[target // 2], p_rsem.at[owner // 2], seq_dev(target)
        )

    def scan_states():
        @pl.when(me < slices)
        def _():
            def one(c, state):
                @pl.when((c != chip) & (c > 0))
                def _():
                    p_out[c] = state.astype(BF16)
                    p_copy(me, 2 * c + core).start()

                @pl.when(c == chip)
                def _():
                    p_in[:, lane(me)] = state.astype(BF16)

                @pl.when((c != chip) & (c < chips - 1))
                def _():
                    remote(t_out.at[0], t_in.at[c], t_ssem.at[0], t_rsem.at[c], seq_dev(me)).wait_recv()

                block = t_in[c].astype(F32)
                total = block[NSTATE : NSTATE + 1] + block[NSTATE + 1 : NSTATE + 2] + block[NSTATE + 2 : NSTATE + 3]
                return jnp.exp(-total) * state + block[:NSTATE]

            lax.fori_loop(0, chips, one, jnp.zeros((NSTATE, LANES), F32))

    def h_copy(j):
        return remote(p_in.at[:, lane(j)], p_in.at[:, lane(j)], h_sem.at[0, j], h_sem.at[1, j], seq_dev(sibling))

    def states_in(q):
        @pl.when(after_first)
        def _():
            @pl.loop(q * TILES, (q + 1) * TILES)
            def _(j):
                @pl.when(j % 2 == core)
                def _():
                    @pl.when(j != me)
                    def _():
                        p_copy(j, me).wait_recv()

                    h_copy(j).start()

            @pl.loop(q * TILES, (q + 1) * TILES)
            def _(j):
                @pl.when(j % 2 != core)
                def _():
                    h_copy(j).wait_recv()

    def init_states():
        @pl.when(jnp.logical_not(after_first))
        def _():
            p_in[...] = jnp.zeros_like(p_in)

    def local_y(q):
        t, r = row_i, col_i % HEAD_P
        left_half = col_i < HEAD_P

        @pl.loop(q * TILES, (q + 1) * TILES)
        def _(j):
            sl = lane(j)
            cx = cumx[:, sl]
            xs = x_ref[:, sl].astype(F32)
            mixes, blocks = [], []
            for part in range(2):
                rows = slice(part * HEAD_P, (part + 1) * HEAD_P)
                here = jnp.sum(
                    jnp.where(row_i[:HEAD_P] == r[:HEAD_P], cx[rows], 0.0), axis=0, keepdims=True
                )
                decay = jnp.exp(jnp.minimum(here - cx, 0.0))
                mixes.append(jnp.where(t >= r + part * HEAD_P, gmat[part] * decay, 0.0))
                blocks.append(jnp.where(left_half[:HEAD_P], xs[rows], 0.0))
                blocks.append(jnp.where(left_half[:HEAD_P], 0.0, xs[rows]))
            mixing = jnp.concatenate(mixes, axis=1).astype(BF16)
            inner = dot(mixing, jnp.concatenate(blocks, axis=0).astype(BF16))
            y0[:, sl] = inner + dsx[0:1, sl] * xs

    def make_u(q):
        c_only = bc_ref[:, NSTATE:]
        c2 = jnp.concatenate([c_only, c_only], axis=1)
        group = (iota((2 * LANES, LANES), 0) % LANES) // HEAD_P == iota((2 * LANES, LANES), 1) // HEAD_P
        ones = group.astype(F32).astype(BF16)

        @pl.loop(q * TILES, (q + 1) * TILES)
        def _(j):
            sl = lane(j)
            before = p_in[:, sl].astype(F32)
            after = jnp.exp(-s_sib[NSTATE : NSTATE + 1, sl]) * before + s_sib[0:NSTATE, sl]
            hi, lo = halves(jnp.where(first, before, after))
            carried = dot(c2, jnp.concatenate([hi, lo], axis=0))
            y = y0[:, sl] + carried * jnp.exp(-cumx[:, sl])
            hi, lo = halves(y * y)
            meansq = dot(jnp.concatenate([hi, lo], axis=1), ones) * (1.0 / HEAD_P)
            u = (y * lax.rsqrt(meansq + 1e-05) * gain_ref[:, sl]).astype(BF16)
            u_all[:, sl] = u

    lanes_w = {w: iota((ROWS, w), 1) for _, w in WINDOWS}
    heads4 = (iota((16, QUAD), 1) // ATT_DIM == iota((16, QUAD), 0) % 8).astype(F32).astype(BF16)
    scale = ATT_DIM ** (-0.5)
    sub8 = iota((8, LANES), 0)

    def only_head(a, block):
        start, width = WINDOWS[a]
        place = lanes_w[width] + start
        keep = (place >= a * ATT_DIM) & (place < (a + 1) * ATT_DIM)
        return jnp.where(keep, block.astype(F32), 0.0).astype(BF16)

    def joined(parts):
        tiles = []
        for tile in range(TILES):
            value = None
            for a, (start, width) in enumerate(WINDOWS):
                lo = tile * LANES - start
                if lo < 0 or lo >= width:
                    continue
                piece = parts[a][:, lo : lo + LANES]
                if value is None:
                    value = piece
                else:
                    value = jnp.where(col_i[:, :] + tile * LANES < a * ATT_DIM, value, piece)
            tiles.append(value)
        return tiles

    def spread4(rows8):
        hi, lo = halves(rows8)
        return dot(jnp.concatenate([hi, lo], axis=0), heads4, dims=((0,), (0,)))

    def finish(q, attended):
        sl = quad_lanes(q)
        res[:, sl] = (x_ref[:, sl].astype(F32) + u_all[:, sl].astype(F32) + attended).astype(BF16)
        send(
            True,
            remote(res.at[:, sl], out_ref.at[:, sl], out_sem.at[0, q], out_sem.at[1, q], ((sec + 1) % sections, me)),
        )

    def attend_kv(q):
        n = ks.index(q)
        base = q * QUAD
        for w, src in ((0, k_ref), (1, v_ref)):
            kv_buf[n, w, 0:ROWS] = src[:, quad_lanes(q)]
        outs = []
        inverse = jnp.zeros((8, LANES), F32)
        for a, (start, width) in enumerate(WINDOWS):
            mine = only_head(a, u_all[:, pl.ds(base + start, width)])
            score = dot(kv_buf[n, 0, :, start : start + width], mine, dims=((1,), (1,))) * scale + bias_k[...]
            top = jnp.max(score, axis=0, keepdims=True)
            expo = jnp.exp(score - top)
            inverse = jnp.where(sub8 == a, 1.0 / jnp.sum(expo, axis=0, keepdims=True), inverse)
            outs.append(dot(expo.astype(BF16), kv_buf[n, 1, :, start : start + width], dims=((0,), (0,))))
        finish(q, jnp.concatenate(joined(outs), axis=1) * spread4(inverse))

    def q_slot(n, d):
        return q_buf.at[n, pl.ds(d * ROWS, ROWS)]

    def q_copy(n, src, d, kind, device):
        return remote(src, q_slot(n, d), q_sem.at[0, n, kind], q_sem.at[1, n, kind], seq_dev(device))

    def q_start(q):
        n = qs.index(q)
        own = u_all.at[:, quad_lanes(q)]
        send(dn2, q_copy(n, own, 2, 0, left))
        send(second, q_copy(n, own, 1, 2, sibling))

    def q_near(q):
        n = qs.index(q)
        near = q_slot(n, 2)
        at(up2, q_copy(n, near, 2, 0, left).wait_recv)
        send(up2 & dn2, q_copy(n, near, 4, 1, left))
        send(up2 & second, q_copy(n, near, 3, 3, sibling))
        send(up2 & first, q_copy(n, near, 1, 2, sibling))

    def q_far(q):
        n = qs.index(q)
        far = q_slot(n, 4)
        at(up4, q_copy(n, far, 4, 1, left).wait_recv)
        send(up4 & first, q_copy(n, far, 3, 3, sibling))

    def q_last(q):
        n = qs.index(q)
        at(first | up2, q_copy(n, q_slot(n, 1), 1, 2, sibling).wait_recv)
        at((first & up2) | (second & up4), q_copy(n, q_slot(n, 3), 3, 3, sibling).wait_recv)

    def sib_copies(n, d, slot, kind):
        rows = pl.ds(d * ROWS, ROWS)
        return [
            remote(
                part_o.at[n, rows], sib_o.at[n, slot], sib_sem.at[0, n, kind, 0], sib_sem.at[1, n, kind, 0],
                seq_dev(sibling),
            ),
            remote(
                part_s.at[n, d], sib_s.at[n, slot], sib_sem.at[0, n, kind, 1], sib_sem.at[1, n, kind, 1],
                seq_dev(sibling),
            ),
        ]

    def partials(q):
        n = qs.index(q)
        base = q * QUAD
        q_buf[n, 0:ROWS] = u_all[:, quad_lanes(q)]

        @pl.loop(0, BACK + 1)
        def _(d):
            rows = pl.ds(pl.multiple_of(d * ROWS, ROWS), ROWS)
            outs = []
            tops, sums = jnp.zeros((8, LANES), F32), jnp.zeros((8, LANES), F32)
            for a, (start, width) in enumerate(WINDOWS):
                key = only_head(a, k_ref[:, pl.ds(base + start, width)])
                score = dot(key, q_buf[n, rows, start : start + width], dims=((1,), (1,))) * scale + bias_q[d]
                top = jnp.maximum(jnp.max(score, axis=0, keepdims=True), LOWEST)
                expo = jnp.exp(score - top)
                tops = jnp.where(sub8 == a, top, tops)
                sums = jnp.where(sub8 == a, jnp.sum(expo, axis=0, keepdims=True), sums)
                outs.append(dot(expo.astype(BF16), v_ref[:, pl.ds(base + start, width)], dims=((0,), (0,))))
            for tile, value in enumerate(joined(outs)):
                part_o[n, rows, tile * LANES : (tile + 1) * LANES] = value.astype(BF16)
            part_s[n, d, 0:8] = tops
            part_s[n, d, 8:16] = sums

        for kind, d in enumerate((1, 3)):
            for copy in sib_copies(n, d, core + kind, kind):
                send(True, copy)

    def sib_wait(q):
        n = qs.index(q)
        for kind, d in enumerate((1, 3)):
            for copy in sib_copies(n, d, 1 - core + kind, kind):
                copy.wait_recv()

    def merged(parts, final=False):
        top = functools.reduce(jnp.maximum, [s[0:8] for _, s in parts])
        weights = [jnp.exp(s[0:8] - top) for _, s in parts]
        total = sum(w * s[8:16] for w, (_, s) in zip(weights, parts))
        if final:
            inverse = jnp.where(sub8 < 4, 1.0 / jnp.where(sub8 < 4, total, 1.0), 0.0)
            weights = [w * inverse for w in weights]
        value = sum(spread4(w) * o.astype(F32) for w, (o, _) in zip(weights, parts))
        return value, top, total

    def part(n, d):
        return part_o[n, d * ROWS : (d + 1) * ROWS], part_s[n, d]

    def chain_copies(n, kind):
        src, srcs, dst, dsts = ((f_out, f_outs, f_in, f_ins), (n_out, n_outs, n_in, n_ins))[kind]
        return [
            remote(src.at[n], dst.at[n], chain_sem.at[0, n, kind, 0], chain_sem.at[1, n, kind, 0], seq_dev(right)),
            remote(srcs.at[n], dsts.at[n], chain_sem.at[0, n, kind, 1], chain_sem.at[1, n, kind, 1], seq_dev(right)),
        ]

    def send_far(q):
        n = qs.index(q)
        sib_wait(q)
        value, top, total = merged([part(n, 4), (sib_o[n, 2], sib_s[n, 2])])
        f_out[n] = value.astype(BF16)
        f_outs[n, 0:8] = top
        f_outs[n, 8:16] = total
        for copy in chain_copies(n, 0):
            send(up4, copy)

    def send_near(q):
        n = qs.index(q)
        for copy in chain_copies(n, 0):
            at(dn2 & up2, copy.wait_recv)
        value, top, total = merged([part(n, 2), (sib_o[n, 1], sib_s[n, 1]), (f_in[n], f_ins[n])])
        n_out[n] = value.astype(BF16)
        n_outs[n, 0:8] = top
        n_outs[n, 8:16] = total
        for copy in chain_copies(n, 1):
            send(up2, copy)

    def finish_q(q):
        n = qs.index(q)
        for copy in chain_copies(n, 1):
            at(dn2, copy.wait_recv)
        value, _, _ = merged([part(n, 0), (sib_o[n, 0], sib_s[n, 0]), (n_in[n], n_ins[n])], final=True)
        finish(q, value)

    def blank_results():
        nothing = jnp.where(iota((16, LANES), 0) < 8, LOWEST, 0.0)

        @pl.loop(0, len(qs))
        def _(n):
            @pl.when(first)
            def _():
                sib_o[n, 0] = jnp.zeros((ROWS, QUAD), BF16)
                sib_s[n, 0] = nothing

            @pl.when(second)
            def _():
                sib_o[n, 2] = jnp.zeros((ROWS, QUAD), BF16)
                sib_s[n, 2] = nothing

            @pl.when(jnp.logical_not(dn2))
            def _():
                f_in[n] = jnp.zeros((ROWS, QUAD), BF16)
                f_ins[n] = nothing
                n_in[n] = jnp.zeros((ROWS, QUAD), BF16)
                n_ins[n] = nothing

    def masks():
        for copy in seg_copies:
            copy.wait_recv()
        own = jnp.broadcast_to(seg_out[0:1], (ROWS, LANES))
        own_col = own.T
        for d in range(BACK + 1):
            if d == 0:
                keep_q = keep_k = (own_col == own) & (row_i <= col_i)
            else:
                other_q = jnp.broadcast_to(seg_q[d - 1, 0:1], (ROWS, LANES))
                other_k = jnp.broadcast_to(seg_k[d - 1, 0:1], (ROWS, LANES)).T
                keep_q = (own_col == other_q) & (me + d < peers)
                keep_k = (other_k == own) & (me >= d)
            bias_q[d] = jnp.where(keep_q, 0.0, MASKED)
            bias_k[d * ROWS : (d + 1) * ROWS] = jnp.where(keep_k, 0.0, MASKED)

    for q in range(quads):
        states_out(q)
    b_only = bc_ref[:, :NSTATE]
    c_only = bc_ref[:, NSTATE:]
    for part_no in range(2):
        rows = b_only[part_no * HEAD_P : (part_no + 1) * HEAD_P]
        gmat[part_no] = dot(c_only, jnp.concatenate([rows, rows], axis=0), dims=((1,), (1,)))
    init_states()
    local_y(0)
    scan_states()
    for q in range(1, quads):
        local_y(q)
    masks()
    if qs:
        blank_results()
    for q in ks:
        kv_near(q)

    order = qs + ks
    for place, q in enumerate(order):
        states_in(q)
        make_u(q)
        if q in qs:
            if place:
                q_near(qs[place - 1])
            q_start(q)
    for q in ks:
        kv_far(q)
    for place, q in enumerate(qs):
        if place == len(qs) - 1:
            q_near(q)
        q_far(q)
        q_last(q)
        partials(q)
        send_far(q)
        if place >= 1:
            send_near(qs[place - 1])
        if place >= 2:
            finish_q(qs[place - 2])
    for q in ks:
        kv_last(q)
        attend_kv(q)
    if qs:
        send_near(qs[-1])
        for q in qs[-2:]:
            finish_q(q)

    for q in range(quads):
        sl = quad_lanes(q)
        remote(res.at[:, sl], out_ref.at[:, sl], out_sem.at[0, q], out_sem.at[1, q], (sec, me)).wait_recv()
    for cond, copy in pending:
        at(cond, copy.wait_send)

    @pl.loop(0, slices)
    def _(j):
        @pl.when(j % 2 == core)
        def _():
            @pl.when(before_last & (j != me))
            def _():
                t_copy(j).wait_send()

            @pl.when(after_first)
            def _():
                h_copy(j).wait_send()

    @pl.when(me < slices)
    def _():
        @pl.loop(1, chips)
        def _(c):
            @pl.when(c != chip)
            def _():
                p_copy(me, 2 * c + core).wait_send()


def layer(modes, sections, peers, x, k, v, bc, rates, dskip, gain, seg):
    quads = len(modes)
    width = quads * QUAD
    slices = quads * TILES
    owned = (slices + 1) // 2
    chips = peers // 2
    nq = max(1, modes.count("q"))
    nk = max(1, modes.count("k"))
    dma = pltpu.SemaphoreType.DMA
    block = (ROWS, QUAD)
    scratch = [
        pltpu.VMEM((ROWS, width), F32),
        pltpu.VMEM((ROWS, width), F32),
        pltpu.VMEM((8, width), F32),
        pltpu.VMEM((2, ROWS, LANES), F32),
        pltpu.VMEM((NSTATE + 8, width), F32),
        pltpu.VMEM((NSTATE + 8, width), F32),
        pltpu.VMEM((owned, NSTATE + 16, LANES), BF16),
        pltpu.VMEM((chips, NSTATE + 16, LANES), BF16),
        pltpu.VMEM((chips, NSTATE, LANES), BF16),
        pltpu.VMEM((NSTATE, width), BF16),
        pltpu.VMEM((ROWS, width), BF16),
        pltpu.VMEM((8, LANES), F32),
        pltpu.VMEM((BACK, 8, LANES), F32),
        pltpu.VMEM((BACK, 8, LANES), F32),
        pltpu.VMEM((SPAN, LANES), F32),
        pltpu.VMEM((BACK + 1, ROWS, LANES), F32),
        pltpu.VMEM((nk, 2, SPAN, QUAD), BF16),
        pltpu.VMEM((nq, SPAN, QUAD), BF16),
        pltpu.VMEM((nq, SPAN, QUAD), BF16),
        pltpu.VMEM((nq, BACK + 1, 16, LANES), F32),
        pltpu.VMEM((nq, 3) + block, BF16),
        pltpu.VMEM((nq, 3, 16, LANES), F32),
    ]
    for _ in range(4):
        scratch += [pltpu.VMEM((nq,) + block, BF16), pltpu.VMEM((nq, 16, LANES), F32)]
    scratch += [
        pltpu.VMEM((ROWS, width), BF16),
        dma((4, BACK)),
        dma((2, quads)),
        dma((owned,)),
        dma((chips,)),
        dma((chips,)),
        dma((owned,)),
        dma((2, slices)),
        dma((2, nk, 2, 4)),
        dma((2, nq, 4)),
        dma((2, nq, 2, 2)),
        dma((2, nq, 2, 2)),
        dma((2, quads)),
    ]
    vmem = pl.BlockSpec(memory_space=pltpu.VMEM)
    return pl.pallas_call(
        functools.partial(kernel, modes, sections, peers),
        out_shape=jax.ShapeDtypeStruct((ROWS, width), BF16),
        in_specs=[vmem] * 8,
        out_specs=pl.BlockSpec(memory_space=pl.ANY),
        scratch_shapes=scratch,
        compiler_params=pltpu.CompilerParams(
            collective_id=0, has_side_effects=True, vmem_limit_bytes=56 * 1024 * 1024
        ),
        name="layer",
    )(x, k, v, bc, rates, dskip, gain, seg)


def build(mesh, modes):
    sections, peers = mesh.shape["section"], mesh.shape["seq"]

    def body(stream, keys, values, bc, rates, dskip, norm_gain, seg_ids):
        out = layer(
            modes, sections, peers,
            stream[0], keys[0], values[0], bc[0], rates[0], dskip, norm_gain, seg_ids,
        )
        return out[None]

    rows = P("section", "seq", None)
    return jax.shard_map(
        body,
        mesh=mesh,
        in_specs=(rows, rows, rows, rows, rows, P("section", None), P("section", None), P("section", "seq")),
        out_specs=rows,
        check_vma=False,
    )


def solution(mesh):
    return build(mesh, MODES)
```

time: 467 us -> 145 us (0.31)
  the two profiles are of different devices: /device:TPU:249 before, /device:TPU:26 now
where the time goes in v1:
time: 145 us; the launch traced here: 144 us
  Pallas kernels  141 us (97%)
  local copies, waits for them, and re-layouts  3.64 us (3%)
    pallas_call x1, Pallas kernels, layer(): pl.pallas_call(functools.partial(kernel, modes, sections, peers), out_sha...  141 us
    unnamed x2, local copies, waits for them, and re-layouts  3.64 us

profile of v1, /device:TPU:26, one launch (start us, length us, event | category | flops | bytes accessed | tf_op | source)
XLA Modules:
  0.0 144.4 jit_solution(2811457003262205932)
XLA Ops:
  0.0 1.5 %copy.9 = f32[1,128,56]{2,1,0:T(8,128)} copy(f32[1,128,56]{1,2,0:T(8,128)} %param.12) | data formatting | bytes 57344 | tf_op args[4]
  1.5 140.8 %layer.1 = bf16[128,3584]{1,0:T(8,128)(2,1)} custom-call(bf16[128,3584]{1,0:T(8,128)(2,1)} %bitcast.7, bf16[128,3584]{1,0:T(8,128)(2,1)} %bitcast.8, bf16[128,3584]{1,0:T(8,128)(2,1)} %bitcast.9, bf16[128,128]{1,0:T(8,128)(2,1)} %bitcast.11, f32[128,56]{1,0:T(8,128)} %bitcast.10, f32[1,56]{1,0:T(1,128)} %dskip_ref.1, f32[1,3584]{1,0:T(1,128)} %gain_ref.1, ...), custom_call_target="tpu_custom_call" | custom-call | tf_op jit(solution)/shard_map/layer/pallas_call | solution.py:671
  142.3 2.2 %copy.11 = bf16[1,128,3584]{2,1,0:T(8,128)(2,1)} copy(bf16[1,128,3584]{2,1,0:T(8,128)(2,1)} %bitcast.6) | data formatting | bytes 1835008
